TPU v7x, 32 devices: a whole 2x2x4 slice. The times are simulated.
32 devices in a mesh: groups: 2 (over y), context: 4 (over z), tensor: 4 (over x, core).
Axes of the slice: x: 2, y: 2, z: 4, core: 2. Of those that a mesh axis runs over, the one named last changes fastest.
Arguments:
- inputs: bfloat16 [4096, 1024], P(('groups', 'context')), parts along dimension 0, may hold values from -6 to 6
- frame_valid: int32 [4096], P(('groups', 'context')), parts along dimension 0, may hold values from 0 to 1, as said below
- norm1_gain: float32 [1024], replicated, may hold values from 0.1 to 1.9
- w_query: bfloat16 [1024, 1024], P(None, 'tensor')
- w_key: bfloat16 [1024, 1024], P(None, 'tensor')
- w_value: bfloat16 [1024, 1024], P(None, 'tensor'), may hold values from -0.1875 to 0.1875
- w_out: bfloat16 [1024, 1024], P('tensor'), may hold values from -0.1875 to 0.1875
- norm2_gain: float32 [1024], replicated, may hold values from 0.1 to 1.9
- w_point1: bfloat16 [2, 1024, 1024], P(None, None, 'tensor'), may hold values from -0.1875 to 0.1875
- w_depth: float32 [31, 1024], P(None, 'tensor'), may hold values from -1.5 to 1.5
- bn_scale: float32 [1024], P('tensor'), may hold values from 0.1 to 1.9
- bn_shift: float32 [1024], P('tensor'), may hold values from -1 to 1
- w_point2: bfloat16 [1024, 1024], P('tensor'), may hold values from -0.1875 to 0.1875
Outputs:
- output: bfloat16 [4096, 1024], P(('groups', 'context', 'tensor')), parts along dimension 0
There are 2 independent parts, one for each index of `groups`. A program takes and returns all parts, laid end to end along the dimension named above; an argument that names none is the same for every part. Nothing has to cross between parts.
Inputs may be any that keep to these rules, and one draw needn't show every extreme that they name: `frame_valid`: the transcript frames form a prefix of the window of at least 1024 frames, followed by at least one padded frame.
All inputs are finite; a program needn't handle non-finite values.
Results may differ from a plain program's by a relative error of at most 0.0095.
Values may be sent and summed in bfloat16 or wider, within the bound.
A program may use at most 64 MiB of HBM per device.

v0:
```python
import math
import jax
import jax.numpy as jnp
from jax import lax
from jax.sharding import PartitionSpec as P

HD = 64
NEG = -1e30


def with_halo(block, sides, width):
    for axis, dim in sides:
        count = lax.axis_size(axis)
        forward = [(i, i + 1) for i in range(count - 1)]
        backward = [(target, source) for source, target in forward]
        low = lax.ppermute(
            lax.slice_in_dim(block, block.shape[dim] - width, None, axis=dim), axis, forward
        )
        high = lax.ppermute(lax.slice_in_dim(block, 0, width, axis=dim), axis, backward)
        block = jnp.concatenate([low, block, high], axis=dim)
    return block


def normalize(rows, gain):
    values = rows.astype(jnp.float32)
    center = jnp.mean(values, axis=-1, keepdims=True)
    spread = jnp.mean(jnp.square(values - center), axis=-1, keepdims=True)
    return ((values - center) * lax.rsqrt(spread + 1e-05) * gain).astype(jnp.bfloat16)


def local(
    inputs,
    frame_valid,
    norm1_gain,
    w_query,
    w_key,
    w_value,
    w_out,
    norm2_gain,
    w_point1,
    w_depth,
    bn_scale,
    bn_shift,
    w_point2,
):
    frames = inputs.shape[0]
    local_cols = w_query.shape[1]
    head_dim = HD
    heads_here = local_cols // head_dim
    scale = 1.0 / math.sqrt(head_dim)
    normed = normalize(inputs, norm1_gain)
    query = jnp.dot(normed, w_query, preferred_element_type=jnp.float32).astype(jnp.bfloat16)
    query = query.reshape(frames, heads_here, head_dim)
    keys = jnp.dot(normed, w_key, preferred_element_type=jnp.float32).astype(jnp.bfloat16)
    vals = jnp.dot(normed, w_value, preferred_element_type=jnp.float32).astype(jnp.bfloat16)

    def update(carry, key_blk, val_blk, valid_blk):
        run_max, run_sum, accum = carry
        rows = key_blk.shape[0]
        key_heads = key_blk.reshape(rows, heads_here, head_dim)
        val_heads = val_blk.reshape(rows, heads_here, head_dim)
        scores = (
            jnp.einsum("qhd,khd->hqk", query, key_heads, preferred_element_type=jnp.float32) * scale
        )
        live = (valid_blk > 0)[None, None, :]
        scores = jnp.where(live, scores, NEG)
        new_max = jnp.maximum(run_max, jnp.max(scores, axis=-1))
        weights = jnp.where(live, jnp.exp(scores - new_max[:, :, None]), 0.0)
        factor = jnp.exp(run_max - new_max)
        run_sum = run_sum * factor + jnp.sum(weights, axis=-1)
        mixed = jnp.einsum(
            "hqk,khd->qhd",
            weights.astype(jnp.bfloat16),
            val_heads,
            preferred_element_type=jnp.float32,
        )
        accum = accum * jnp.repeat(factor.T, head_dim, axis=1) + mixed.reshape(frames, local_cols)
        return (new_max, run_sum, accum)

    def visit(carry, key_blk, val_blk, valid_blk):
        return update(carry, key_blk, val_blk, valid_blk)

    start_state = (
        jnp.full((heads_here, frames), NEG, jnp.float32),
        jnp.zeros((heads_here, frames), jnp.float32),
        jnp.zeros((frames, local_cols), jnp.float32),
    )
    carry = start_state
    key_part = lax.all_gather(keys, "context", axis=0, tiled=True)
    val_part = lax.all_gather(vals, "context", axis=0, tiled=True)
    valid_part = lax.all_gather(frame_valid, "context", axis=0, tiled=True)
    rows = key_part.shape[0]
    shards = max(rows // frames, 1)
    group = math.gcd(shards, max(1536 // frames, 1))
    blocks = shards // group
    block_rows = rows // blocks

    def advance(state, items):
        return (visit(state, items[0], items[1], items[2]), None)

    stacked = (
        key_part.reshape(blocks, block_rows, local_cols),
        val_part.reshape(blocks, block_rows, local_cols),
        valid_part.reshape(blocks, block_rows),
    )
    carry, unused = lax.scan(advance, carry, stacked)
    run_max, run_sum, accum = carry
    attended = (accum / jnp.repeat(run_sum.T, head_dim, axis=1)).astype(jnp.bfloat16)
    share = frames // lax.axis_size("tensor")
    first_row = lax.axis_index("tensor") * share
    total = lax.psum(jnp.dot(attended, w_out, preferred_element_type=jnp.float32), "tensor")
    residual = (inputs.astype(jnp.float32) + total).astype(jnp.bfloat16)
    normed_two = normalize(residual, norm2_gain)
    residual_rows = lax.dynamic_slice_in_dim(residual, first_row, share, 0)
    value_half = jnp.dot(normed_two, w_point1[0], preferred_element_type=jnp.float32)
    gate_half = jnp.dot(normed_two, w_point1[1], preferred_element_type=jnp.float32)
    gated = jnp.where(
        (frame_valid > 0)[:, None], value_half * jax.nn.sigmoid(gate_half), 0.0
    ).astype(jnp.bfloat16)
    taps = w_depth.shape[0]
    half = (taps - 1) // 2
    padded = with_halo(gated, (("context", 0),), half)
    depth = jnp.zeros((frames, gated.shape[1]), jnp.float32)
    for tap in range(taps):
        depth = depth + padded[tap : tap + frames].astype(jnp.float32) * w_depth[tap]
    activated = jax.nn.silu(depth * bn_scale + bn_shift).astype(jnp.bfloat16)
    conv_rows = lax.psum_scatter(
        jnp.dot(activated, w_point2, preferred_element_type=jnp.float32).astype(jnp.bfloat16),
        "tensor",
        scatter_dimension=0,
        tiled=True,
    ).astype(jnp.float32)
    return (residual_rows.astype(jnp.float32) + conv_rows).astype(jnp.bfloat16)


def solution(mesh):
    placed = (
        P(("groups", "context"), None),
        P(("groups", "context")),
        P(),
        P(None, "tensor"),
        P(None, "tensor"),
        P(None, "tensor"),
        P("tensor", None),
        P(),
        P(None, None, "tensor"),
        P(None, "tensor"),
        P("tensor"),
        P("tensor"),
        P("tensor", None),
    )
    return jax.shard_map(
        local,
        mesh=mesh,
        in_specs=placed,
        out_specs=P(("groups", "context", "tensor"), None),
        check_vma=False,
    )
```

profile of v0, /device:TPU:0, one launch (start us, length us, event | category | flops | bytes accessed | tf_op | source)
XLA Modules:
  0.0 218.2 jit_solution(7202695658550756041)
XLA Ops:
  6.6 1.6 convert_reduce_fusion
  8.2 1.6 fusion.17
  9.9 1.2 convolution_convert_fusion.3
  11.2 1.2 convolution_convert_fusion.1
  12.5 13.7 %all-gather = s32[4,1,512]{2,1,0:T(1,128)S(1)} all-gather(s32[1,1,512]{2,1,0:T(1,128)S(1)} %bitcast.111), channel_id=1, replica_groups=mesh['groups'=2,'context'=4,'tensor'=4] {'context'}, dimensions={0}, use_global_device_ids=true | all-gather | bytes 10240 | tf_op jit(solution)/shard_map/all_gather | solution.py:91
  26.2 1.7 convolution_convert_fusion.2
  27.9 14.0 %all-gather.4.cloned.1.call-done = bf16[2048,256]{1,0:T(8,128)(2,1)} async-done(((bf16[512,256]{1,0:T(8,128)(2,1)}), bf16[2048,256]{1,0:T(8,128)(2,1)}) %all-gather.4.cloned.1.call-update) | async-done | bytes 1048592 | tf_op jit(solution)/shard_map/all_gather | solution.py:89
  41.9 29.0 %all-gather.6.cloned.1.call-done = bf16[2048,256]{1,0:T(8,128)(2,1)} async-done(((bf16[512,256]{1,0:T(8,128)(2,1)}), bf16[2048,256]{1,0:T(8,128)(2,1)}) %all-gather.6.cloned.1.call-update) | async-done | bytes 1048592 | tf_op jit(solution)/shard_map/all_gather | solution.py:90
  70.9 44.4 %while.15 = (s32[]{:T(128)}, f32[4,512]{1,0:T(4,128)S(1)}, f32[4,512]{1,0:T(4,128)S(1)}, f32[512,256]{0,1:T(8,128)S(1)}, s32[4,512]{1,0:T(4,128)S(1)}, /*index=5...) while((s32[]{:T(128)}, f32[4,512]{1,0:T(4,128)S(1)}, ...), condition=%wide.region_5.6_spmd.clone, body=%wide.region_2.5_spmd.clone.sunk | while | flops 282472960 | bytes 17698944 | solution.py:106
  72.2 2.9 %bitcast_reduce_fusion.2 = (f32[4,512]{1,0:T(4,128)S(1)}, f32[4,512,512]{2,1,0:T(8,128)}) fusion(pred[512]{0:T(512)(128)(4,1)S(1)} %compare_reduce_fusion.2, bf16[512,4,64]{0,2,1:T(8,128)(2,1)S(1)} %bitcast.104, bf16[512,4,64]{0,2,1:T(8,128)(2,1)S(1)} %get-tuple-element.237), kind=kOutput, calls=%fused_computation.1.clone.1 | convolution fusion | flops 137361408 | bytes 4727296 | tf_op jit(solution)/shard_map/while/body/eval_jaxpr/qhd,khd->hqk/dot_general | solution.py:63
  75.1 3.3 %fusion.96 = f32[4,512]{1,0:T(4,128)S(1)} fusion(f32[4,512,512]{2,1,0:T(8,128)} %get-tuple-element.208, f32[4,512]{1,0:T(4,128)S(1)} %get-tuple-element.232, pred[512]{0:T(512)(128)(4,1)S(1)} %compare_reduce_fusion.2), kind=kLoop, calls=%fused_computation.6.clone.1 | loop fusion | flops 5240832 | bytes 4211200 | tf_op jit(solution)/shard_map/while/body/eval_jaxpr/reduce_sum | solution.py:70
  78.6 3.3 %fusion.98 = f32[4,64,512]{2,1,0:T(8,128)S(1)} fusion(bf16[512,4,64]{0,2,1:T(8,128)(2,1)S(1)} %bitcast.106, f32[4,512,512]{2,1,0:T(8,128)} %get-tuple-element.208, f32[4,512]{1,0:T(4,128)S(1)} %get-tuple-element.232, pred[512]{0:T(512)(128)(4,1)S(1)} %compare_reduce_fusion.2), kind=kOutput, calls=%fused_computation.7.clone.1 | convolution fusion | flops 139460608 | bytes 4989440 | tf_op jit(solution)/shard_map/while/body/eval_jaxpr/hqk,khd->qhd/dot_general | solution.py:71
  82.1 1.1 constant_dynamic-slice_fusion.3
  83.3 2.9 %bitcast_reduce_fusion.2 = (f32[4,512]{1,0:T(4,128)S(1)}, f32[4,512,512]{2,1,0:T(8,128)}) fusion(pred[512]{0:T(512)(128)(4,1)S(1)} %compare_reduce_fusion.2, bf16[512,4,64]{0,2,1:T(8,128)(2,1)S(1)} %bitcast.104, bf16[512,4,64]{0,2,1:T(8,128)(2,1)S(1)} %get-tuple-element.237), kind=kOutput, calls=%fused_computation.1.clone.1 | convolution fusion | flops 137361408 | bytes 4727296 | tf_op jit(solution)/shard_map/while/body/eval_jaxpr/qhd,khd->hqk/dot_general | solution.py:63
  86.2 3.3 %fusion.96 = f32[4,512]{1,0:T(4,128)S(1)} fusion(f32[4,512,512]{2,1,0:T(8,128)} %get-tuple-element.208, f32[4,512]{1,0:T(4,128)S(1)} %get-tuple-element.232, pred[512]{0:T(512)(128)(4,1)S(1)} %compare_reduce_fusion.2), kind=kLoop, calls=%fused_computation.6.clone.1 | loop fusion | flops 5240832 | bytes 4211200 | tf_op jit(solution)/shard_map/while/body/eval_jaxpr/reduce_sum | solution.py:70
  89.7 3.3 %fusion.98 = f32[4,64,512]{2,1,0:T(8,128)S(1)} fusion(bf16[512,4,64]{0,2,1:T(8,128)(2,1)S(1)} %bitcast.106, f32[4,512,512]{2,1,0:T(8,128)} %get-tuple-element.208, f32[4,512]{1,0:T(4,128)S(1)} %get-tuple-element.232, pred[512]{0:T(512)(128)(4,1)S(1)} %compare_reduce_fusion.2), kind=kOutput, calls=%fused_computation.7.clone.1 | convolution fusion | flops 139460608 | bytes 4989440 | tf_op jit(solution)/shard_map/while/body/eval_jaxpr/hqk,khd->qhd/dot_general | solution.py:71
  93.2 1.1 constant_dynamic-slice_fusion.3
  94.4 2.9 %bitcast_reduce_fusion.2 = (f32[4,512]{1,0:T(4,128)S(1)}, f32[4,512,512]{2,1,0:T(8,128)}) fusion(pred[512]{0:T(512)(128)(4,1)S(1)} %compare_reduce_fusion.2, bf16[512,4,64]{0,2,1:T(8,128)(2,1)S(1)} %bitcast.104, bf16[512,4,64]{0,2,1:T(8,128)(2,1)S(1)} %get-tuple-element.237), kind=kOutput, calls=%fused_computation.1.clone.1 | convolution fusion | flops 137361408 | bytes 4727296 | tf_op jit(solution)/shard_map/while/body/eval_jaxpr/qhd,khd->hqk/dot_general | solution.py:63
  97.3 3.3 %fusion.96 = f32[4,512]{1,0:T(4,128)S(1)} fusion(f32[4,512,512]{2,1,0:T(8,128)} %get-tuple-element.208, f32[4,512]{1,0:T(4,128)S(1)} %get-tuple-element.232, pred[512]{0:T(512)(128)(4,1)S(1)} %compare_reduce_fusion.2), kind=kLoop, calls=%fused_computation.6.clone.1 | loop fusion | flops 5240832 | bytes 4211200 | tf_op jit(solution)/shard_map/while/body/eval_jaxpr/reduce_sum | solution.py:70
  100.8 3.3 %fusion.98 = f32[4,64,512]{2,1,0:T(8,128)S(1)} fusion(bf16[512,4,64]{0,2,1:T(8,128)(2,1)S(1)} %bitcast.106, f32[4,512,512]{2,1,0:T(8,128)} %get-tuple-element.208, f32[4,512]{1,0:T(4,128)S(1)} %get-tuple-element.232, pred[512]{0:T(512)(128)(4,1)S(1)} %compare_reduce_fusion.2), kind=kOutput, calls=%fused_computation.7.clone.1 | convolution fusion | flops 139460608 | bytes 4989440 | tf_op jit(solution)/shard_map/while/body/eval_jaxpr/hqk,khd->qhd/dot_general | solution.py:71
  105.5 2.9 %bitcast_reduce_fusion.2 = (f32[4,512]{1,0:T(4,128)S(1)}, f32[4,512,512]{2,1,0:T(8,128)}) fusion(pred[512]{0:T(512)(128)(4,1)S(1)} %compare_reduce_fusion.2, bf16[512,4,64]{0,2,1:T(8,128)(2,1)S(1)} %bitcast.104, bf16[512,4,64]{0,2,1:T(8,128)(2,1)S(1)} %get-tuple-element.237), kind=kOutput, calls=%fused_computation.1.clone.1 | convolution fusion | flops 137361408 | bytes 4727296 | tf_op jit(solution)/shard_map/while/body/eval_jaxpr/qhd,khd->hqk/dot_general | solution.py:63
  108.4 3.3 %fusion.96 = f32[4,512]{1,0:T(4,128)S(1)} fusion(f32[4,512,512]{2,1,0:T(8,128)} %get-tuple-element.208, f32[4,512]{1,0:T(4,128)S(1)} %get-tuple-element.232, pred[512]{0:T(512)(128)(4,1)S(1)} %compare_reduce_fusion.2), kind=kLoop, calls=%fused_computation.6.clone.1 | loop fusion | flops 5240832 | bytes 4211200 | tf_op jit(solution)/shard_map/while/body/eval_jaxpr/reduce_sum | solution.py:70
  111.9 3.3 %fusion.98 = f32[4,64,512]{2,1,0:T(8,128)S(1)} fusion(bf16[512,4,64]{0,2,1:T(8,128)(2,1)S(1)} %bitcast.106, f32[4,512,512]{2,1,0:T(8,128)} %get-tuple-element.208, f32[4,512]{1,0:T(4,128)S(1)} %get-tuple-element.232, pred[512]{0:T(512)(128)(4,1)S(1)} %compare_reduce_fusion.2), kind=kOutput, calls=%fused_computation.7.clone.1 | convolution fusion | flops 139460608 | bytes 4989440 | tf_op jit(solution)/shard_map/while/body/eval_jaxpr/hqk,khd->qhd/dot_general | solution.py:71
  115.4 1.8 fusion.73
  117.4 50.9 %all-reduce.2.cloned.1.call-done = f32[512,1024]{1,0:T(8,128)} async-done(((f32[512,1024]{1,0:T(8,128)}), f32[512,1024]{1,0:T(8,128)}) %all-reduce.2.cloned.1.call-update) | async-done | bytes 2097168 | tf_op jit(solution)/shard_map/psum | solution.py:111
  168.3 2.0 convert_reduce_fusion.1
  171.9 1.3 collective-permute-start.1
  173.2 4.5 %collective-permute-start = (bf16[15,256]{1,0:T(8,128)(2,1)S(1)}, bf16[15,256]{1,0:T(8,128)(2,1)S(1)}, u32[]{:S(2)}, u32[]{:S(2)}) collective-permute-start(bf16[15,256]{1,0:T(8,128)(2,1)S(1)} %get-tuple-element.117), channel_id=1, source_target_pairs={{0,4},{4,8},{8,12},{1,5},{5,9},{9,13},{2,6},{6,10},{10,14},{3,7},{... | collective-permute-start | bytes 23048 | tf_op jit(solution)/shard_map/ppermute | solution.py:16
  177.7 1.3 collective-permute-done
  179.1 4.9 %convolution_convert_fusion = bf16[512,1024]{1,0:T(8,128)(2,1)} fusion(bf16[256,1024]{1,0:T(8,128)(2,1)S(1)} %copy-done.7, bf16[512,256]{1,0:T(8,128)(2,1)S(1)} %fusion.28, bf16[15,256]{1,0:T(8,128)(2,1)S(1)} %collective-permute-done.1, bf16[15,256]{1,0:T(8,128)(2,1)S(1)} %collective-permute-done, f32[256]{0:T(256)S(1)} %copy-done.10, ...), kind=kOutput, calls=%fused_computation.67 | convolution fusion | flops 293732352 | bytes 1884160 | tf_op jit(solution)/shard_map/dot_general | solution.py:128
  184.0 26.0 %reduce-scatter.2.cloned.1.call-done = bf16[128,1024]{1,0:T(8,128)(2,1)} async-done(((bf16[512,1024]{1,0:T(8,128)(2,1)}), bf16[128,1024]{1,0:T(8,128)(2,1)}) %reduce-scatter.2.cloned.1.call-update) | async-done | bytes 262160 | tf_op jit(solution)/shard_map/reduce_scatter | solution.py:127
  209.9 1.7 add_convert_fusion
  (79 shorter events, 6.1 us)
Async XLA Ops:
  6.5 108.9 %copy-start = (bf16[256,1024]{1,0:T(8,128)(2,1)S(1)}, bf16[256,1024]{1,0:T(8,128)(2,1)}, u32[]{:S(2)}) copy-start(bf16[256,1024]{1,0:T(8,128)(2,1)} %param.21) | copy-start | bytes 1572868
  6.5 3.3 %copy-start.1 = (bf16[512,1024]{1,0:T(8,128)(2,1)S(1)}, bf16[512,1024]{1,0:T(8,128)(2,1)}, u32[]{:S(2)}) copy-start(bf16[512,1024]{1,0:T(8,128)(2,1)} %param.15) | copy-start | bytes 3145732
  6.5 3.3 %copy-start.5 = (bf16[1024,256]{1,0:T(8,128)(2,1)S(1)}, bf16[1024,256]{1,0:T(8,128)(2,1)}, u32[]{:S(2)}) copy-start(bf16[1024,256]{1,0:T(8,128)(2,1)} %param.19) | copy-start | bytes 1572868
  6.5 3.3 %copy-start.8 = (f32[1024]{0:T(1024)S(1)}, f32[1024]{0:T(1024)}, u32[]{:S(2)}) copy-start(f32[1024]{0:T(1024)} %param.17) | copy-start | bytes 12292
  6.5 35.4 %all-gather.4.cloned.1.call-start = ((), (), s32[]{:S(2)}) async-start(), calls=%async_computation.1 | async-start | bytes 1310720 | tf_op jit(solution)/shard_map/all_gather | solution.py:89
  9.8 1.4 copy-start.6
  11.1 1.4 copy-start.3
  11.1 59.8 %all-gather.6.cloned.1.call-start = ((), (), s32[]{:S(2)}) async-start(), calls=%async_computation.2 | async-start | bytes 1310720 | tf_op jit(solution)/shard_map/all_gather | solution.py:90
  12.4 155.9 %all-reduce.2.cloned.1.call-start = ((), (), s32[]{:S(2)}) async-start(), calls=%async_computation.3 | async-start | bytes 4194304 | tf_op jit(solution)/shard_map/psum | solution.py:111
  115.4 1.9 copy-start.2
  117.2 92.7 %reduce-scatter.2.cloned.1.call-start = ((), (), s32[]{:S(2)}) async-start(), calls=%async_computation.4 | async-start | bytes 1310720 | tf_op jit(solution)/shard_map/reduce_scatter | solution.py:127
  117.3 53.4 %copy-start.9 = (f32[1024]{0:T(1024)S(1)}, f32[1024]{0:T(1024)}, u32[]{:S(2)}) copy-start(f32[1024]{0:T(1024)} %param.22) | copy-start | bytes 12292
  168.3 2.4 %copy-start.4 = (bf16[2,1024,256]{2,1,0:T(8,128)(2,1)S(1)}, bf16[2,1024,256]{2,1,0:T(8,128)(2,1)}, u32[]{:S(2)}) copy-start(bf16[2,1024,256]{2,1,0:T(8,128)(2,1)} %param.23) | copy-start | bytes 3145732
  171.3 7.8 %copy-start.7 = (bf16[256,1024]{1,0:T(8,128)(2,1)S(1)}, bf16[256,1024]{1,0:T(8,128)(2,1)}, u32[]{:S(2)}) copy-start(bf16[256,1024]{1,0:T(8,128)(2,1)} %param.27) | copy-start | bytes 1572868
  171.3 7.8 %copy-start.10 = (f32[256]{0:T(256)S(1)}, f32[256]{0:T(256)}, u32[]{:S(2)}) copy-start(f32[256]{0:T(256)} %param.26) | copy-start | bytes 3076
  171.3 7.8 %copy-start.11 = (f32[256]{0:T(256)S(1)}, f32[256]{0:T(256)}, u32[]{:S(2)}) copy-start(f32[256]{0:T(256)} %param.25) | copy-start | bytes 3076
  171.9 5.9 %collective-permute-start.1 = (bf16[15,256]{1,0:T(8,128)(2,1)S(1)}, bf16[15,256]{1,0:T(8,128)(2,1)S(1)}, u32[]{:S(2)}, u32[]{:S(2)}) collective-permute-start(bf16[15,256]{1,0:T(8,128)(2,1)S(1)} %get-tuple-element.118), channel_id=1, source_target_pairs={{4,0},{8,4},{12,8},{5,1},{9,5},{13,9},{6,2},{10,6},{14,10},{7,3},{... | collective-permute-start | bytes 23048 | tf_op jit(solution)/shard_map/ppermute | solution.py:19
  173.2 5.9 %collective-permute-start = (bf16[15,256]{1,0:T(8,128)(2,1)S(1)}, bf16[15,256]{1,0:T(8,128)(2,1)S(1)}, u32[]{:S(2)}, u32[]{:S(2)}) collective-permute-start(bf16[15,256]{1,0:T(8,128)(2,1)S(1)} %get-tuple-element.117), channel_id=1, source_target_pairs={{0,4},{4,8},{8,12},{1,5},{5,9},{9,13},{2,6},{6,10},{10,14},{3,7},{... | collective-permute-start | bytes 23048 | tf_op jit(solution)/shard_map/ppermute | solution.py:16
Sparse Core Ops, SparseCore 0:
  11.2 30.6 all-gather.3
  43.5 27.3 all-gather.5
  117.4 50.8 all-reduce.1
  184.1 25.8 reduce-scatter.1
where the time goes:
time: 219 us; the launch traced here: 218 us
  waiting for transfers between devices  121 us (55%)
  matrix products  36.7 us (17%)
  other arithmetic  21.4 us (10%)
  blocking collectives  13.7 us (6%)
  between operations  13.4 us (6%)
  starting transfers between devices  6 us (3%)
  local copies, waits for them, and re-layouts  5.5 us (3%)
    psum x1, waiting for transfers between devices, local(): lax.psum(jnp.dot(attended, w_out, preferred_element_type=jnp.float32), 't...  50.9 us
    all_gather x1, waiting for transfers between devices, local(): val_part = lax.all_gather(vals, 'context', axis=0, tiled=True)  29 us
    reduce_scatter x1, waiting for transfers between devices, local(): lax.psum_scatter(jnp.dot(activated, w_point2, preferred_element_type=jnp....  26 us
    all_gather x1, waiting for transfers between devices, local(): key_part = lax.all_gather(keys, 'context', axis=0, tiled=True)  14 us
    all_gather x1, blocking collectives, local(): valid_part = lax.all_gather(frame_valid, 'context', axis=0, tiled=True)  13.7 us
    dot_general x4, matrix products, update(): jnp.einsum('hqk,khd->qhd', weights.astype(jnp.bfloat16), val_heads, prefe...  13.1 us
    reduce_sum x4, other arithmetic, update(): run_sum = run_sum * factor + jnp.sum(weights, axis=-1)  13.1 us
    dot_general x4, matrix products, update(): jnp.einsum('qhd,khd->hqk', query, key_heads, preferred_element_type=jnp.f...  11.6 us
  transfers between devices with their start and end apart: 6, of which 5 were waited for; matrix products, arithmetic and copies ran while one was open for 1% of the time, Pallas kernels for 0%

commit v1 on v0

--- a/solution.py
+++ b/solution.py
@@ -108,7 +108,10 @@
     attended = (accum / jnp.repeat(run_sum.T, head_dim, axis=1)).astype(jnp.bfloat16)
     share = frames // lax.axis_size("tensor")
     first_row = lax.axis_index("tensor") * share
-    total = lax.psum(jnp.dot(attended, w_out, preferred_element_type=jnp.float32), "tensor")
+    total = jnp.sum(
+        lax.all_gather(jnp.dot(attended, w_out, preferred_element_type=jnp.float32), "tensor"),
+        axis=0,
+    )
     residual = (inputs.astype(jnp.float32) + total).astype(jnp.bfloat16)
     normed_two = normalize(residual, norm2_gain)
     residual_rows = lax.dynamic_slice_in_dim(residual, first_row, share, 0)

time: 219 us -> 224 us (1.023)
  waiting for transfers between devices: 121 us -> 129 us
  other arithmetic: 21.4 us -> 18.9 us
    all_gather x0 -> x1, waiting for transfers between devices: none -> 57.8 us  [local(): lax.all_gather(jnp.dot(attended, w_out, preferred_element_type=jnp.float3...]
    psum x1 -> x0, waiting for transfers between devices: 50.9 us -> none  [local(): lax.psum(jnp.dot(attended, w_out, preferred_element_type=jnp.float32), 't...]
    reduce_sum x4, other arithmetic: 13.1 us -> 4.64 us  [update(): run_sum = run_sum * factor + jnp.sum(weights, axis=-1)]
    reduce_sum x0 -> x1, other arithmetic: none -> 5.93 us  [local(): jnp.sum(lax.all_gather(jnp.dot(attended, w_out, preferred_element_type=jn...]
    ppermute x1, waiting for transfers between devices: 0.01 us -> 4.2 us  [with_halo(): lax.ppermute(lax.slice_in_dim(block, 0, width, axis=dim), axis, backward)]
where the time goes in v1:
time: 224 us; the launch traced here: 223 us
  waiting for transfers between devices  129 us (58%)
  matrix products  37.4 us (17%)
  other arithmetic  18.9 us (8%)
  blocking collectives  13.7 us (6%)
  between operations  13.4 us (6%)
  local copies, waits for them, and re-layouts  5.52 us (2%)
  starting transfers between devices  4.84 us (2%)
    all_gather x1, waiting for transfers between devices, local(): lax.all_gather(jnp.dot(attended, w_out, preferred_element_type=jnp.float3...  57.8 us
    all_gather x1, waiting for transfers between devices, local(): val_part = lax.all_gather(vals, 'context', axis=0, tiled=True)  29 us
    reduce_scatter x1, waiting for transfers between devices, local(): lax.psum_scatter(jnp.dot(activated, w_point2, preferred_element_type=jnp....  24.1 us
    all_gather x1, waiting for transfers between devices, local(): key_part = lax.all_gather(keys, 'context', axis=0, tiled=True)  14 us
    dot_general x4, matrix products, update(): jnp.einsum('hqk,khd->qhd', weights.astype(jnp.bfloat16), val_heads, prefe...  13.8 us
    all_gather x1, blocking collectives, local(): valid_part = lax.all_gather(frame_valid, 'context', axis=0, tiled=True)  13.7 us
    dot_general x4, matrix products, update(): jnp.einsum('qhd,khd->hqk', query, key_heads, preferred_element_type=jnp.f...  11.6 us
    reduce_sum x1, other arithmetic, local(): jnp.sum(lax.all_gather(jnp.dot(attended, w_out, preferred_element_type=jn...  5.93 us
  transfers between devices with their start and end apart: 6, of which 5 were waited for; matrix products, arithmetic and copies ran while one was open for 1% of the time, Pallas kernels for 0%

profile of v1, /device:TPU:0, one launch (start us, length us, event | category | flops | bytes accessed | tf_op | source)
XLA Modules:
  0.0 223.3 jit_solution(12946484165938280765)
XLA Ops:
  6.6 1.6 convert_reduce_fusion
  8.2 1.6 fusion.17
  9.9 1.2 convolution_convert_fusion.3
  11.2 1.2 convolution_convert_fusion.1
  12.5 13.7 %all-gather.1 = s32[4,1,512]{2,1,0:T(1,128)S(1)} all-gather(s32[1,1,512]{2,1,0:T(1,128)S(1)} %bitcast.113), channel_id=1, replica_groups=mesh['groups'=2,'context'=4,'tensor'=4] {'context'}, dimensions={0}, use_global_device_ids=true | all-gather | bytes 10240 | tf_op jit(solution)/shard_map/all_gather | solution.py:91
  26.2 1.7 convolution_convert_fusion.2
  27.9 14.0 %all-gather.6.cloned.1.call-done = bf16[2048,256]{1,0:T(8,128)(2,1)} async-done(((bf16[512,256]{1,0:T(8,128)(2,1)}), bf16[2048,256]{1,0:T(8,128)(2,1)}) %all-gather.6.cloned.1.call-update) | async-done | bytes 1048592 | tf_op jit(solution)/shard_map/all_gather | solution.py:89
  41.9 29.0 %all-gather.8.cloned.1.call-done = bf16[2048,256]{1,0:T(8,128)(2,1)} async-done(((bf16[512,256]{1,0:T(8,128)(2,1)}), bf16[2048,256]{1,0:T(8,128)(2,1)}) %all-gather.8.cloned.1.call-update) | async-done | bytes 1048592 | tf_op jit(solution)/shard_map/all_gather | solution.py:90
  70.9 36.7 %while.15 = (s32[]{:T(128)}, f32[4,512]{1,0:T(4,128)S(1)}, f32[4,512]{1,0:T(4,128)S(1)}, f32[512,256]{0,1:T(8,128)S(1)}, s32[4,512]{1,0:T(4,128)S(1)}, /*index=5...) while((s32[]{:T(128)}, f32[4,512]{1,0:T(4,128)S(1)}, ...), condition=%wide.region_5.6_spmd.clone, body=%wide.region_2.5_spmd.clone.sunk | while | flops 282472960 | bytes 34476180 | solution.py:106
  72.2 2.9 %bitcast_reduce_fusion.2 = (f32[4,512]{1,0:T(4,128)S(1)}, f32[4,512,512]{2,1,0:T(8,128)}) fusion(pred[512]{0:T(512)(128)(4,1)S(1)} %compare_reduce_fusion.2, bf16[512,4,64]{0,2,1:T(8,128)(2,1)S(1)} %bitcast.105, bf16[512,4,64]{0,2,1:T(8,128)(2,1)S(1)} %get-tuple-element.237), kind=kOutput, calls=%fused_computation.1.clone.1 | convolution fusion | flops 137361408 | bytes 4727296 | tf_op jit(solution)/shard_map/while/body/eval_jaxpr/qhd,khd->hqk/dot_general | solution.py:63
  75.3 3.4 %fusion.98 = f32[4,64,512]{2,1,0:T(8,128)S(1)} fusion(bf16[512,4,64]{0,2,1:T(8,128)(2,1)S(1)} %bitcast.108, f32[4,512,512]{2,1,0:T(8,128)} %get-tuple-element.208, f32[4,512]{1,0:T(4,128)S(1)} %get-tuple-element.232, pred[512]{0:T(512)(128)(4,1)S(1)} %compare_reduce_fusion.2), kind=kOutput, calls=%fused_computation.7.clone.1 | convolution fusion | flops 139460608 | bytes 4989440 | tf_op jit(solution)/shard_map/while/body/eval_jaxpr/hqk,khd->qhd/dot_general | solution.py:71
  78.9 1.2 fusion.96
  80.1 1.1 constant_dynamic-slice_fusion.3
  81.4 2.9 %bitcast_reduce_fusion.2 = (f32[4,512]{1,0:T(4,128)S(1)}, f32[4,512,512]{2,1,0:T(8,128)}) fusion(pred[512]{0:T(512)(128)(4,1)S(1)} %compare_reduce_fusion.2, bf16[512,4,64]{0,2,1:T(8,128)(2,1)S(1)} %bitcast.105, bf16[512,4,64]{0,2,1:T(8,128)(2,1)S(1)} %get-tuple-element.237), kind=kOutput, calls=%fused_computation.1.clone.1 | convolution fusion | flops 137361408 | bytes 4727296 | tf_op jit(solution)/shard_map/while/body/eval_jaxpr/qhd,khd->hqk/dot_general | solution.py:63
  84.4 3.4 %fusion.98 = f32[4,64,512]{2,1,0:T(8,128)S(1)} fusion(bf16[512,4,64]{0,2,1:T(8,128)(2,1)S(1)} %bitcast.108, f32[4,512,512]{2,1,0:T(8,128)} %get-tuple-element.208, f32[4,512]{1,0:T(4,128)S(1)} %get-tuple-element.232, pred[512]{0:T(512)(128)(4,1)S(1)} %compare_reduce_fusion.2), kind=kOutput, calls=%fused_computation.7.clone.1 | convolution fusion | flops 139460608 | bytes 4989440 | tf_op jit(solution)/shard_map/while/body/eval_jaxpr/hqk,khd->qhd/dot_general | solution.py:71
  88.1 1.2 fusion.96
  90.5 2.9 %bitcast_reduce_fusion.2 = (f32[4,512]{1,0:T(4,128)S(1)}, f32[4,512,512]{2,1,0:T(8,128)}) fusion(pred[512]{0:T(512)(128)(4,1)S(1)} %compare_reduce_fusion.2, bf16[512,4,64]{0,2,1:T(8,128)(2,1)S(1)} %bitcast.105, bf16[512,4,64]{0,2,1:T(8,128)(2,1)S(1)} %get-tuple-element.237), kind=kOutput, calls=%fused_computation.1.clone.1 | convolution fusion | flops 137361408 | bytes 4727296 | tf_op jit(solution)/shard_map/while/body/eval_jaxpr/qhd,khd->hqk/dot_general | solution.py:63
  93.6 3.4 %fusion.98 = f32[4,64,512]{2,1,0:T(8,128)S(1)} fusion(bf16[512,4,64]{0,2,1:T(8,128)(2,1)S(1)} %bitcast.108, f32[4,512,512]{2,1,0:T(8,128)} %get-tuple-element.208, f32[4,512]{1,0:T(4,128)S(1)} %get-tuple-element.232, pred[512]{0:T(512)(128)(4,1)S(1)} %compare_reduce_fusion.2), kind=kOutput, calls=%fused_computation.7.clone.1 | convolution fusion | flops 139460608 | bytes 4989440 | tf_op jit(solution)/shard_map/while/body/eval_jaxpr/hqk,khd->qhd/dot_general | solution.py:71
  97.2 1.2 fusion.96
  99.7 2.9 %bitcast_reduce_fusion.2 = (f32[4,512]{1,0:T(4,128)S(1)}, f32[4,512,512]{2,1,0:T(8,128)}) fusion(pred[512]{0:T(512)(128)(4,1)S(1)} %compare_reduce_fusion.2, bf16[512,4,64]{0,2,1:T(8,128)(2,1)S(1)} %bitcast.105, bf16[512,4,64]{0,2,1:T(8,128)(2,1)S(1)} %get-tuple-element.237), kind=kOutput, calls=%fused_computation.1.clone.1 | convolution fusion | flops 137361408 | bytes 4727296 | tf_op jit(solution)/shard_map/while/body/eval_jaxpr/qhd,khd->hqk/dot_general | solution.py:63
  102.8 3.4 %fusion.98 = f32[4,64,512]{2,1,0:T(8,128)S(1)} fusion(bf16[512,4,64]{0,2,1:T(8,128)(2,1)S(1)} %bitcast.108, f32[4,512,512]{2,1,0:T(8,128)} %get-tuple-element.208, f32[4,512]{1,0:T(4,128)S(1)} %get-tuple-element.232, pred[512]{0:T(512)(128)(4,1)S(1)} %compare_reduce_fusion.2), kind=kOutput, calls=%fused_computation.7.clone.1 | convolution fusion | flops 139460608 | bytes 4989440 | tf_op jit(solution)/shard_map/while/body/eval_jaxpr/hqk,khd->qhd/dot_general | solution.py:71
  106.4 1.2 fusion.96
  107.7 1.8 fusion.73
  109.7 57.8 %all-gather.10.cloned.1.call-done = f32[2048,1024]{1,0:T(8,128)} async-done(((f32[512,1024]{1,0:T(8,128)}), f32[2048,1024]{1,0:T(8,128)}) %all-gather.10.cloned.1.call-update) | async-done | bytes 8388624 | tf_op jit(solution)/shard_map/all_gather | solution.py:112
  167.5 5.9 %reduce_sum.56 = f32[512,1024]{1,0:T(8,128)} reduce(f32[4,512,1024]{2,1,0:T(8,128)} %bitcast.106, f32[]{:T(128)} %constant.17.clone.1), dimensions={0}, to_apply=%region_6.7 | reduce | flops 1572864 | bytes 10485764 | tf_op jit(solution)/shard_map/reduce_sum | solution.py:111
  173.4 2.0 convert_reduce_fusion.1
  177.0 3.4 %collective-permute-start = (bf16[15,256]{1,0:T(8,128)(2,1)S(1)}, bf16[15,256]{1,0:T(8,128)(2,1)S(1)}, u32[]{:S(2)}, u32[]{:S(2)}) collective-permute-start(bf16[15,256]{1,0:T(8,128)(2,1)S(1)} %get-tuple-element.117), channel_id=1, source_target_pairs={{0,4},{4,8},{8,12},{1,5},{5,9},{9,13},{2,6},{6,10},{10,14},{3,7},{... | collective-permute-start | bytes 23048 | tf_op jit(solution)/shard_map/ppermute | solution.py:16
  180.4 1.3 collective-permute-start.1
  181.7 4.2 %collective-permute-done.1 = bf16[15,256]{1,0:T(8,128)(2,1)S(1)} collective-permute-done((bf16[15,256]{1,0:T(8,128)(2,1)S(1)}, bf16[15,256]{1,0:T(8,128)(2,1)S(1)}, u32[]{:S(2)}, u32[]{:S(2)}) %collective-permute-start.1) | collective-permute-done | bytes 7712 | tf_op jit(solution)/shard_map/ppermute | solution.py:19
  185.9 4.9 %convolution_convert_fusion = bf16[512,1024]{1,0:T(8,128)(2,1)} fusion(bf16[256,1024]{1,0:T(8,128)(2,1)S(1)} %copy-done.8, bf16[512,256]{1,0:T(8,128)(2,1)S(1)} %fusion.28, bf16[15,256]{1,0:T(8,128)(2,1)S(1)} %collective-permute-done.1, bf16[15,256]{1,0:T(8,128)(2,1)S(1)} %collective-permute-done, f32[256]{0:T(256)S(1)} %copy-done.11, ...), kind=kOutput, calls=%fused_computation.67 | convolution fusion | flops 293732352 | bytes 1884160 | tf_op jit(solution)/shard_map/dot_general | solution.py:131
  190.9 24.1 %reduce-scatter.2.cloned.1.call-done = bf16[128,1024]{1,0:T(8,128)(2,1)} async-done(((bf16[512,1024]{1,0:T(8,128)(2,1)}), bf16[128,1024]{1,0:T(8,128)(2,1)}) %reduce-scatter.2.cloned.1.call-update) | async-done | bytes 262160 | tf_op jit(solution)/shard_map/reduce_scatter | solution.py:130
  215.0 1.7 add_convert_fusion
  (88 shorter events, 7.2 us)
Async XLA Ops:
  6.5 101.1 %copy-start = (bf16[256,1024]{1,0:T(8,128)(2,1)S(1)}, bf16[256,1024]{1,0:T(8,128)(2,1)}, u32[]{:S(2)}) copy-start(bf16[256,1024]{1,0:T(8,128)(2,1)} %param.21) | copy-start | bytes 1572868
  6.5 3.3 %copy-start.2 = (bf16[512,1024]{1,0:T(8,128)(2,1)S(1)}, bf16[512,1024]{1,0:T(8,128)(2,1)}, u32[]{:S(2)}) copy-start(bf16[512,1024]{1,0:T(8,128)(2,1)} %param.15) | copy-start | bytes 3145732
  6.5 3.3 %copy-start.9 = (f32[1024]{0:T(1024)S(1)}, f32[1024]{0:T(1024)}, u32[]{:S(2)}) copy-start(f32[1024]{0:T(1024)} %param.17) | copy-start | bytes 12292
  6.5 3.3 %copy-start.6 = (bf16[1024,256]{1,0:T(8,128)(2,1)S(1)}, bf16[1024,256]{1,0:T(8,128)(2,1)}, u32[]{:S(2)}) copy-start(bf16[1024,256]{1,0:T(8,128)(2,1)} %param.19) | copy-start | bytes 1572868
  6.5 35.4 %all-gather.6.cloned.1.call-start = ((), (), s32[]{:S(2)}) async-start(), calls=%async_computation.1 | async-start | bytes 1310720 | tf_op jit(solution)/shard_map/all_gather | solution.py:89
  9.8 1.4 copy-start.7
  11.1 1.4 copy-start.4
  11.1 59.8 %all-gather.8.cloned.1.call-start = ((), (), s32[]{:S(2)}) async-start(), calls=%async_computation.2 | async-start | bytes 1310720 | tf_op jit(solution)/shard_map/all_gather | solution.py:90
  12.4 155.1 %all-gather.10.cloned.1.call-start = ((), (), s32[]{:S(2)}) async-start(), calls=%async_computation.4 | async-start | bytes 10485760 | tf_op jit(solution)/shard_map/all_gather | solution.py:112
  75.2 3.6 %copy-start.1 = (f32[4,512,512]{2,1,0:T(8,128)S(1)}, f32[4,512,512]{2,1,0:T(8,128)}, u32[]{:S(2)}) copy-start(f32[4,512,512]{2,1,0:T(8,128)} %get-tuple-element.208) | copy-start | bytes 12582916 | tf_op jit(solution)/shard_map/while
  84.4 3.6 %copy-start.1 = (f32[4,512,512]{2,1,0:T(8,128)S(1)}, f32[4,512,512]{2,1,0:T(8,128)}, u32[]{:S(2)}) copy-start(f32[4,512,512]{2,1,0:T(8,128)} %get-tuple-element.208) | copy-start | bytes 12582916 | tf_op jit(solution)/shard_map/while
  93.6 3.6 %copy-start.1 = (f32[4,512,512]{2,1,0:T(8,128)S(1)}, f32[4,512,512]{2,1,0:T(8,128)}, u32[]{:S(2)}) copy-start(f32[4,512,512]{2,1,0:T(8,128)} %get-tuple-element.208) | copy-start | bytes 12582916 | tf_op jit(solution)/shard_map/while
  102.8 3.6 %copy-start.1 = (f32[4,512,512]{2,1,0:T(8,128)S(1)}, f32[4,512,512]{2,1,0:T(8,128)}, u32[]{:S(2)}) copy-start(f32[4,512,512]{2,1,0:T(8,128)} %get-tuple-element.208) | copy-start | bytes 12582916 | tf_op jit(solution)/shard_map/while
  107.7 1.9 copy-start.3
  109.6 105.5 %reduce-scatter.2.cloned.1.call-start = ((), (), s32[]{:S(2)}) async-start(), calls=%async_computation.3 | async-start | bytes 1310720 | tf_op jit(solution)/shard_map/reduce_scatter | solution.py:130
  173.4 2.4 %copy-start.5 = (bf16[2,1024,256]{2,1,0:T(8,128)(2,1)S(1)}, bf16[2,1024,256]{2,1,0:T(8,128)(2,1)}, u32[]{:S(2)}) copy-start(bf16[2,1024,256]{2,1,0:T(8,128)(2,1)} %param.23) | copy-start | bytes 3145732
  173.4 2.4 %copy-start.10 = (f32[1024]{0:T(1024)S(1)}, f32[1024]{0:T(1024)}, u32[]{:S(2)}) copy-start(f32[1024]{0:T(1024)} %param.22) | copy-start | bytes 12292
  176.4 9.5 %copy-start.8 = (bf16[256,1024]{1,0:T(8,128)(2,1)S(1)}, bf16[256,1024]{1,0:T(8,128)(2,1)}, u32[]{:S(2)}) copy-start(bf16[256,1024]{1,0:T(8,128)(2,1)} %param.27) | copy-start | bytes 1572868
  176.4 9.5 %copy-start.11 = (f32[256]{0:T(256)S(1)}, f32[256]{0:T(256)}, u32[]{:S(2)}) copy-start(f32[256]{0:T(256)} %param.26) | copy-start | bytes 3076
  176.4 9.5 %copy-start.12 = (f32[256]{0:T(256)S(1)}, f32[256]{0:T(256)}, u32[]{:S(2)}) copy-start(f32[256]{0:T(256)} %param.25) | copy-start | bytes 3076
  177.0 4.7 %collective-permute-start = (bf16[15,256]{1,0:T(8,128)(2,1)S(1)}, bf16[15,256]{1,0:T(8,128)(2,1)S(1)}, u32[]{:S(2)}, u32[]{:S(2)}) collective-permute-start(bf16[15,256]{1,0:T(8,128)(2,1)S(1)} %get-tuple-element.117), channel_id=1, source_target_pairs={{0,4},{4,8},{8,12},{1,5},{5,9},{9,13},{2,6},{6,10},{10,14},{3,7},{... | collective-permute-start | bytes 23048 | tf_op jit(solution)/shard_map/ppermute | solution.py:16
  180.4 5.5 %collective-permute-start.1 = (bf16[15,256]{1,0:T(8,128)(2,1)S(1)}, bf16[15,256]{1,0:T(8,128)(2,1)S(1)}, u32[]{:S(2)}, u32[]{:S(2)}) collective-permute-start(bf16[15,256]{1,0:T(8,128)(2,1)S(1)} %get-tuple-element.118), channel_id=1, source_target_pairs={{4,0},{8,4},{12,8},{5,1},{9,5},{13,9},{6,2},{10,6},{14,10},{7,3},{... | collective-permute-start | bytes 23048 | tf_op jit(solution)/shard_map/ppermute | solution.py:19
Sparse Core Ops, SparseCore 0:
  11.2 30.6 all-gather.5
  43.5 27.3 all-gather.7
  109.7 57.7 all-gather.9
  191.0 23.9 reduce-scatter.1
